TPU v7x, 32 devices: a whole 2x2x4 slice. The times are simulated.
32 devices in a mesh: row: 4 (over x, core), col: 8 (over z, y).
Axes of the slice: x: 2, y: 2, z: 4, core: 2. Of those that a mesh axis runs over, the one named last changes fastest.
Arguments:
- row_points: bfloat16 [64, 64, 256], P('row'), may hold values from -25.5 to 25.5
- col_points: bfloat16 [32, 64, 256], P('col'), may hold values from -25.5 to 25.5
- block_lists: int32 [64, 16], P('row'), may hold values from 0 to 31, as said below
Outputs:
- row_potential: float32 [64, 256], P('row')
- col_potential: float32 [32, 256], P('col')
Inputs may be any that keep to these rules, and one draw needn't show every extreme that they name: `block_lists`: the 16 column blocks of a row block are distinct. Among the row blocks of one index of row, at most 64 list entries name column blocks of one index of col, and exactly 64 for some index of col. Every column block is named by some row block of every index of row.
All inputs are finite; a program needn't handle non-finite values.
Results may differ from a plain program's by a relative error of at most 0.0003.
Values sent between devices are 32-bit elements; how exact they have to be, the bound alone decides.
A program may use at most 64 MiB of HBM per device.

v0:
```python
import math

import jax
import jax.numpy as jnp
from jax import lax
from jax.sharding import PartitionSpec as P

DIM = 64
ITERS = 4
CAPACITY = 64


eps_reg = 0.05
neg_big = -1e30
group_slots = 8


def tile_partials(
    row_points, col_points, row_norms, col_norms, row_index, col_index, biases, over_columns
):
    row_tiles = row_points[row_index]
    col_tiles = col_points[col_index]
    inner_prod = jnp.einsum(
        "sdp,sdq->spq", row_tiles, col_tiles, preferred_element_type=jnp.float32
    )
    cost_tile = (
        row_norms[row_index][:, :, None] + col_norms[col_index][:, None, :] - 2.0 * inner_prod
    ) / DIM
    if over_columns:
        scores = (biases[:, None, :] - cost_tile) / eps_reg
        reduce_axis = 2
    else:
        scores = (biases[:, :, None] - cost_tile) / eps_reg
        reduce_axis = 1
    peak_vals = jnp.max(scores, axis=reduce_axis)
    totals = jnp.sum(jnp.exp(scores - jnp.expand_dims(peak_vals, reduce_axis)), axis=reduce_axis)
    return (peak_vals, totals)


def slot_partials(
    row_points, col_points, row_norms, col_norms, row_slot, col_slot, biases, over_columns
):
    groups = row_slot.shape[0] // group_slots
    block_size = row_points.shape[2]

    def one_group(members):
        return tile_partials(
            row_points,
            col_points,
            row_norms,
            col_norms,
            members[0],
            members[1],
            members[2],
            over_columns,
        )

    peak_parts, sum_parts = lax.map(
        one_group,
        (
            row_slot.reshape(groups, group_slots),
            col_slot.reshape(groups, group_slots),
            biases.reshape(groups, group_slots, block_size),
        ),
    )
    return (peak_parts.reshape(-1, block_size), sum_parts.reshape(-1, block_size))


def block_combine(peak_parts, sum_parts, members, slot_block, usable):
    block_peak = jnp.max(jnp.where(members[:, :, None], peak_parts[None, :, :], neg_big), axis=1)
    scale = jnp.where(usable[:, None], jnp.exp(peak_parts - block_peak[slot_block]), 0.0)
    block_sum = jnp.dot(
        members.astype(jnp.float32), sum_parts * scale, precision=lax.Precision.HIGHEST
    )
    return (block_peak, block_sum)


def potential_from(peak_vals, totals, log_mass):
    return eps_reg * (log_mass - (peak_vals + jnp.log(totals)))


def body(row_points, col_points, block_lists):
    row_blocks_here = row_points.shape[0]
    col_blocks_here = col_points.shape[0]
    block_size = row_points.shape[2]
    row_mass = -math.log(lax.axis_size("row") * row_blocks_here * block_size)
    col_mass = -math.log(lax.axis_size("col") * col_blocks_here * block_size)
    row_norms = jnp.sum(jnp.square(row_points.astype(jnp.float32)), axis=1)
    col_norms = jnp.sum(jnp.square(col_points.astype(jnp.float32)), axis=1)
    owned = (block_lists // col_blocks_here == lax.axis_index("col")).reshape(-1)
    entry_rank = jnp.cumsum(owned.astype(jnp.int32)) - 1
    slot_list = jnp.arange(CAPACITY, dtype=jnp.int32)
    picked = owned[None, :] & (entry_rank[None, :] == slot_list[:, None])
    entries = jnp.arange(owned.shape[0], dtype=jnp.int32)
    entry_of_slot = jnp.sum(jnp.where(picked, entries[None, :], 0), axis=1)
    usable = jnp.any(picked, axis=1)
    row_slot = entry_of_slot // block_lists.shape[1]
    col_slot = block_lists.reshape(-1)[entry_of_slot] % col_blocks_here
    row_members = (row_slot[None, :] == jnp.arange(row_blocks_here)[:, None]) & usable[None, :]
    col_members = (col_slot[None, :] == jnp.arange(col_blocks_here)[:, None]) & usable[None, :]
    col_potential = jnp.zeros((col_blocks_here, block_size), jnp.float32)
    row_potential = jnp.zeros((row_blocks_here, block_size), jnp.float32)
    for sweep in range(ITERS):
        peak_parts, sum_parts = slot_partials(
            row_points,
            col_points,
            row_norms,
            col_norms,
            row_slot,
            col_slot,
            col_potential[col_slot],
            True,
        )
        block_peak, block_sum = block_combine(peak_parts, sum_parts, row_members, row_slot, usable)
        whole_peak = lax.pmax(block_peak, "col")
        whole_sum = lax.psum(block_sum * jnp.exp(block_peak - whole_peak), "col")
        row_potential = potential_from(whole_peak, whole_sum, row_mass)
        peak_parts, sum_parts = slot_partials(
            row_points,
            col_points,
            row_norms,
            col_norms,
            row_slot,
            col_slot,
            row_potential[row_slot],
            False,
        )
        block_peak, block_sum = block_combine(peak_parts, sum_parts, col_members, col_slot, usable)
        whole_peak = lax.pmax(block_peak, "row")
        whole_sum = lax.psum(block_sum * jnp.exp(block_peak - whole_peak), "row")
        col_potential = potential_from(whole_peak, whole_sum, col_mass)
    return (row_potential, col_potential)


def solution(mesh):
    placed = (P("row", None, None), P("col", None, None), P("row", None))
    return jax.shard_map(
        body,
        mesh=mesh,
        in_specs=placed,
        out_specs=(P("row", None), P("col", None)),
        check_vma=False,
    )
```

profile of v0, /device:TPU:0, one launch (start us, length us, event | category | flops | bytes accessed | tf_op | source)
XLA Modules:
  0.0 725.8 jit_solution(2049064676753216977)
XLA Ops:
  6.9 48.3 %while.96 = (s32[]{:T(128)}, f32[8,8,256]{2,1,0:T(8,128)S(1)}, f32[8,8,256]{2,1,0:T(8,128)S(1)}, f32[8,8,256]{2,1,0:T(8,128)S(1)}, s32[8,8]{1,0:T(8,128)S(1)}, /...) while((s32[]{:T(128)}, f32[8,8,256]{2,1,0:T(8,128)S(1)}, ...), condition=%wide.region_9.10_spmd, body=%wide.region_6.9_spmd.sunk | while | flops 71825456 | bytes 5906877 | solution.py:58
  6.9 1.6 gather_fusion
  13.0 1.6 gather_fusion
  19.0 1.6 gather_fusion
  25.0 1.6 gather_fusion
  31.1 1.6 gather_fusion
  43.2 1.6 gather_fusion
  49.2 1.6 gather_fusion
  56.3 38.8 %pmax.56 = f32[16,256]{1,0:T(8,128)S(1)} all-reduce(f32[16,256]{1,0:T(8,128)S(1)} %select_reduce_fusion.3), channel_id=1, replica_groups=mesh['row'=4,'col'=8] {'col'}, use_global_device_ids=true, to_apply=%region_11.12 | all-reduce | flops 4096 | bytes 32768 | tf_op jit(solution)/shard_map/pmax | solution.py:115
  95.3 33.0 %psum.56 = f32[16,256]{1,0:T(8,128)S(1)} all-reduce(f32[16,256]{1,0:T(8,128)S(1)} %convolution_multiply_fusion.3), channel_id=1, replica_groups=mesh['row'=4,'col'=8] {'col'}, use_global_device_ids=true, to_apply=%region_12.13 | all-reduce | flops 4096 | bytes 32768 | tf_op jit(solution)/shard_map/psum | solution.py:116
  129.0 48.4 %while.97 = (s32[]{:T(128)}, f32[8,8,256]{2,1,0:T(8,128)S(1)}, f32[8,8,256]{2,1,0:T(8,128)S(1)}, f32[8,8,256]{2,1,0:T(8,128)S(1)}, s32[8,8]{1,0:T(8,128)S(1)}, /...) while((s32[]{:T(128)}, f32[8,8,256]{2,1,0:T(8,128)S(1)}, ...), condition=%wide.region_16.17_spmd, body=%wide.region_13.16_spmd.sunk | while | flops 71825456 | bytes 5906877 | solution.py:58
  129.0 1.6 gather_fusion.4
  178.2 5.7 pmax.57
  184.1 6.6 psum.57
  191.4 48.3 %while.98 = (s32[]{:T(128)}, f32[8,8,256]{2,1,0:T(8,128)S(1)}, f32[8,8,256]{2,1,0:T(8,128)S(1)}, f32[8,8,256]{2,1,0:T(8,128)S(1)}, s32[8,8]{1,0:T(8,128)S(1)}, /...) while((s32[]{:T(128)}, f32[8,8,256]{2,1,0:T(8,128)S(1)}, ...), condition=%wide.region_23.24_spmd, body=%wide.region_20.23_spmd.sunk | while | flops 71825456 | bytes 5906877 | solution.py:58
  240.6 33.0 %pmax.58 = f32[16,256]{1,0:T(8,128)S(1)} all-reduce(f32[16,256]{1,0:T(8,128)S(1)} %select_reduce_fusion.2), channel_id=1, replica_groups=mesh['row'=4,'col'=8] {'col'}, use_global_device_ids=true, to_apply=%region_25.26 | all-reduce | flops 4096 | bytes 32768 | tf_op jit(solution)/shard_map/pmax | solution.py:115
  273.8 33.0 %psum.58 = f32[16,256]{1,0:T(8,128)S(1)} all-reduce(f32[16,256]{1,0:T(8,128)S(1)} %convolution_multiply_fusion.2), channel_id=1, replica_groups=mesh['row'=4,'col'=8] {'col'}, use_global_device_ids=true, to_apply=%region_26.27 | all-reduce | flops 4096 | bytes 32768 | tf_op jit(solution)/shard_map/psum | solution.py:116
  307.5 48.4 %while.99 = (s32[]{:T(128)}, f32[8,8,256]{2,1,0:T(8,128)S(1)}, f32[8,8,256]{2,1,0:T(8,128)S(1)}, f32[8,8,256]{2,1,0:T(8,128)S(1)}, s32[8,8]{1,0:T(8,128)S(1)}, /...) while((s32[]{:T(128)}, f32[8,8,256]{2,1,0:T(8,128)S(1)}, ...), condition=%wide.region_30.31_spmd, body=%wide.region_27.30_spmd.sunk | while | flops 71825456 | bytes 5906877 | solution.py:58
  356.7 5.7 pmax.59
  362.5 6.2 psum.59
  369.5 48.4 %while.100 = (s32[]{:T(128)}, f32[8,8,256]{2,1,0:T(8,128)S(1)}, f32[8,8,256]{2,1,0:T(8,128)S(1)}, f32[8,8,256]{2,1,0:T(8,128)S(1)}, s32[8,8]{1,0:T(8,128)S(1)}, ...) while((s32[]{:T(128)}, f32[8,8,256]{2,1,0:T(8,128)S(1)}, ...), condition=%wide.region_37.38_spmd, body=%wide.region_34.37_spmd.sunk | while | flops 71825456 | bytes 5906877 | solution.py:58
  418.8 33.0 %pmax.60 = f32[16,256]{1,0:T(8,128)S(1)} all-reduce(f32[16,256]{1,0:T(8,128)S(1)} %select_reduce_fusion.1), channel_id=1, replica_groups=mesh['row'=4,'col'=8] {'col'}, use_global_device_ids=true, to_apply=%region_39.40 | all-reduce | flops 4096 | bytes 32768 | tf_op jit(solution)/shard_map/pmax | solution.py:115
  451.9 33.0 %psum.60 = f32[16,256]{1,0:T(8,128)S(1)} all-reduce(f32[16,256]{1,0:T(8,128)S(1)} %convolution_multiply_fusion.1), channel_id=1, replica_groups=mesh['row'=4,'col'=8] {'col'}, use_global_device_ids=true, to_apply=%region_40.41 | all-reduce | flops 4096 | bytes 32768 | tf_op jit(solution)/shard_map/psum | solution.py:116
  485.6 48.4 %while.101 = (s32[]{:T(128)}, f32[8,8,256]{2,1,0:T(8,128)S(1)}, f32[8,8,256]{2,1,0:T(8,128)S(1)}, f32[8,8,256]{2,1,0:T(8,128)S(1)}, s32[8,8]{1,0:T(8,128)S(1)}, ...) while((s32[]{:T(128)}, f32[8,8,256]{2,1,0:T(8,128)S(1)}, ...), condition=%wide.region_44.45_spmd, body=%wide.region_41.44_spmd.sunk | while | flops 71825456 | bytes 5906877 | solution.py:58
  534.8 5.7 pmax.61
  540.7 6.5 psum.61
  547.9 48.3 %while.102 = (s32[]{:T(128)}, f32[8,8,256]{2,1,0:T(8,128)S(1)}, f32[8,8,256]{2,1,0:T(8,128)S(1)}, f32[8,8,256]{2,1,0:T(8,128)S(1)}, s32[8,8]{1,0:T(8,128)S(1)}, ...) while((s32[]{:T(128)}, f32[8,8,256]{2,1,0:T(8,128)S(1)}, ...), condition=%wide.region_51.52_spmd, body=%wide.region_48.51_spmd.sunk | while | flops 71825456 | bytes 5906877 | solution.py:58
  597.1 33.0 %pmax.62 = f32[16,256]{1,0:T(8,128)S(1)} all-reduce(f32[16,256]{1,0:T(8,128)S(1)} %select_reduce_fusion), channel_id=1, replica_groups=mesh['row'=4,'col'=8] {'col'}, use_global_device_ids=true, to_apply=%region_53.54 | all-reduce | flops 4096 | bytes 32768 | tf_op jit(solution)/shard_map/pmax | solution.py:115
  630.3 33.0 %psum.62 = f32[16,256]{1,0:T(8,128)S(1)} all-reduce(f32[16,256]{1,0:T(8,128)S(1)} %convolution_multiply_fusion), channel_id=1, replica_groups=mesh['row'=4,'col'=8] {'col'}, use_global_device_ids=true, to_apply=%region_54.55 | all-reduce | flops 4096 | bytes 32768 | tf_op jit(solution)/shard_map/psum | solution.py:116
  664.0 48.3 %while.103 = (s32[]{:T(128)}, f32[8,8,256]{2,1,0:T(8,128)S(1)}, f32[8,8,256]{2,1,0:T(8,128)S(1)}, f32[8,8,256]{2,1,0:T(8,128)S(1)}, s32[8,8]{1,0:T(8,128)S(1)}, ...) while((s32[]{:T(128)}, f32[8,8,256]{2,1,0:T(8,128)S(1)}, ...), condition=%wide.region_58.59_spmd, body=%wide.region_55.58_spmd.sunk | while | flops 71825456 | bytes 5906877 | solution.py:58
  713.1 5.7 pmax.63
  719.0 6.2 psum.63
  (845 shorter events, 387.8 us)
Async XLA Ops:
  663.3 0.7 copy-start
where the time goes:
time: 731 us; the launch traced here: 726 us
  blocking collectives  318 us (44%)
  local copies, waits for them, and re-layouts  283 us (39%)
  matrix products  91.3 us (12%)
  other arithmetic  26.6 us (4%)
    pmax x4, blocking collectives, body(): whole_peak = lax.pmax(block_peak, 'col')  138 us
    psum x4, blocking collectives, body(): whole_sum = lax.psum(block_sum * jnp.exp(block_peak - whole_peak), 'col')  132 us
    gather x64, local copies, waits for them, and re-layouts, tile_partials(): row_tiles = row_points[row_index]  103 us
    gather x64, local copies, waits for them, and re-layouts, tile_partials(): col_tiles = col_points[col_index]  94 us
    dot_general x64, matrix products, tile_partials(): jnp.einsum('sdp,sdq->spq', row_tiles, col_tiles, preferred_element_type=j...  89.7 us
    gather x64, local copies, waits for them, and re-layouts, tile_partials(): col_norms[col_index][:, None, :]  36 us
    gather x64, local copies, waits for them, and re-layouts, tile_partials(): row_norms[row_index][:, :, None] + col_norms[col_index][:, None, :]  36 us
    psum x4, blocking collectives, body(): whole_sum = lax.psum(block_sum * jnp.exp(block_peak - whole_peak), 'row')  25.6 us

commit v1 on v0

v1 whole, which is shorter than its diff:
```python
import functools
import math

import jax
import jax.numpy as jnp
from jax import lax
from jax.experimental import pallas as pl
from jax.experimental.pallas import tpu as pltpu
from jax.sharding import PartitionSpec as P

ITERS = 4
eps_reg = 0.05
kappa = math.log2(math.e) / eps_reg
masked_score = -(2.0**40)
depth = 256
slab = 16
MESH = pl.DeviceIdType.MESH


def split3(values):
    high = values.astype(jnp.bfloat16).astype(jnp.float32)
    rest = values - high
    mid = rest.astype(jnp.bfloat16).astype(jnp.float32)
    low = (rest - mid).astype(jnp.bfloat16).astype(jnp.float32)
    return high, mid, low


def with_bias(base, bias, first):
    rows = lax.broadcasted_iota(jnp.int32, base.shape, 0)
    high, mid, low = split3(bias)
    out = jnp.where(rows == first, high, base)
    out = jnp.where(rows == first + 1, mid, out)
    return jnp.where(rows == first + 2, low, out)


def log2_sum(parts):
    peak = jnp.max(parts, axis=0, keepdims=True)
    return peak + jnp.log2(jnp.sum(jnp.exp2(parts - peak), axis=0, keepdims=True))


def kernel(
    n_row, n_col, lists_ref, x_ref, y_ref, f_ref, g_ref,
    a_ref, at_ref, b_ref, bt_ref, abase, bbase, t_ref, u_ref, nx_ref, ny_ref,
    l_ref, rs_recv, lc_ref, c_send, c_recv, s_ref,
    rs_ssem, rs_rsem, ag_ssem, ag_rsem, c_ssem, c_rsem,
):
    me_row = lax.axis_index("row")
    me_col = lax.axis_index("col")
    row_blocks, dim, block = x_ref.shape
    col_blocks = y_ref.shape[0]
    per = row_blocks // n_col
    width = per * block
    cols = col_blocks * block
    log2_a = -math.log2(n_row * row_blocks * block)
    log2_b = -math.log2(n_col * cols)
    alpha = 2.0 * kappa / dim
    beta = kappa / dim

    barrier = pltpu.get_barrier_semaphore()
    for step in range(1, n_col):
        pl.semaphore_signal(
            barrier, inc=1, device_id={"col": lax.rem(me_col + step, n_col)}, device_id_type=MESH
        )
    for step in range(1, n_row):
        pl.semaphore_signal(
            barrier, inc=1, device_id={"row": lax.rem(me_row + step, n_row)}, device_id_type=MESH
        )

    slab_rows = lax.broadcasted_iota(jnp.int32, (slab, block), 0)
    zeros = jnp.zeros((depth - 3 * dim - slab, block), jnp.bfloat16)

    for c in range(col_blocks):
        lanes = pl.ds(c * block, block)
        y = y_ref[c]
        for part in range(3):
            b_ref[pl.ds(part * dim, dim), lanes] = y
        y32 = y.astype(jnp.float32)
        norm = jnp.sum(y32 * y32, axis=0, keepdims=True) * beta
        ny_ref[:, lanes] = norm
        u_ref[:, lanes] = -norm
        base = jnp.where((slab_rows < 3) | (slab_rows == 6 + c), 1.0, 0.0)
        bbase[:, lanes] = base
        b_ref[pl.ds(3 * dim, slab), lanes] = with_bias(base, -norm, 3).astype(jnp.bfloat16)
        b_ref[pl.ds(3 * dim + slab, depth - 3 * dim - slab), lanes] = zeros
        bt_ref[pl.ds(c * block, block), :] = b_ref[:, lanes].T

    def prepare(q, carry):
        for part in range(per):
            r = q * per + part
            lanes = pl.ds(part * block, block)
            x = x_ref[r].astype(jnp.float32)
            norm = jnp.sum(x * x, axis=0, keepdims=True) * beta
            nx_ref[q, :, lanes] = norm
            t_ref[q, :, lanes] = -norm
            for i, piece in enumerate(split3(x * alpha)):
                a_ref[q, pl.ds(i * dim, dim), lanes] = piece.astype(jnp.bfloat16)
            listed = lists_ref[pl.ds(r, 1), :]
            base = jnp.where((slab_rows >= 3) & (slab_rows < 6), 1.0, 0.0)
            for c in range(col_blocks):
                hit = jnp.where(listed == me_col * col_blocks + c, 1.0, 0.0)
                hit = jnp.max(hit, axis=1, keepdims=True)
                fill = jnp.broadcast_to(jnp.where(hit > 0.0, 0.0, masked_score), (slab, block))
                base = jnp.where(slab_rows == 6 + c, fill, base)
            abase[q, :, lanes] = base
            a_ref[q, pl.ds(3 * dim, slab), lanes] = with_bias(base, -norm, 0).astype(jnp.bfloat16)
            a_ref[q, pl.ds(3 * dim + slab, depth - 3 * dim - slab), lanes] = zeros
            at_ref[q, pl.ds(part * block, block), :] = a_ref[q, :, lanes].T
        return carry

    lax.fori_loop(0, n_col, prepare, 0)
    pl.semaphore_wait(barrier, n_col - 1 + n_row - 1)

    def row_part(q):
        points = a_ref[q]
        peak = None
        for c in range(col_blocks):
            scores = jnp.dot(
                bt_ref[pl.ds(c * block, block), :], points, preferred_element_type=jnp.float32
            )
            s_ref[c] = scores
            top = jnp.max(scores.reshape(block // 8, 8, width), axis=0)
            peak = top if peak is None else jnp.maximum(peak, top)
        peak = jnp.max(peak, axis=0, keepdims=True)
        total = jnp.zeros((8, width), jnp.float32)
        for c in range(col_blocks):
            total += jnp.sum(jnp.exp2(s_ref[c] - peak).reshape(block // 8, 8, width), axis=0)
        return peak + jnp.log2(jnp.sum(total, axis=0, keepdims=True))

    def scatter_copy(peer, slot):
        return pltpu.make_async_remote_copy(
            src_ref=l_ref.at[peer], dst_ref=rs_recv.at[slot],
            send_sem=rs_ssem.at[peer], recv_sem=rs_rsem.at[slot],
            device_id={"col": peer}, device_id_type=MESH,
        )

    def gather_copy(peer, slot):
        return pltpu.make_async_remote_copy(
            src_ref=t_ref.at[slot], dst_ref=t_ref.at[slot],
            send_sem=ag_ssem.at[peer], recv_sem=ag_rsem.at[slot],
            device_id={"col": peer}, device_id_type=MESH,
        )

    def col_copy(peer, slot, k):
        return pltpu.make_async_remote_copy(
            src_ref=c_send.at[k], dst_ref=c_recv.at[k, slot],
            send_sem=c_ssem.at[k, peer], recv_sem=c_rsem.at[k, slot],
            device_id={"row": peer}, device_id_type=MESH,
        )

    def iteration(k, carry):
        def row_step(s, c2):
            q = lax.rem(me_col + 1 + s, n_col)
            l_ref[q] = row_part(q)

            @pl.when(s < n_col - 1)
            def _():
                scatter_copy(q, me_col).start()

            return c2

        lax.fori_loop(0, n_col, row_step, 0)
        rs_recv[me_col] = l_ref[me_col]

        def row_wait(s, c2):
            scatter_copy(me_col, lax.rem(me_col + 1 + s, n_col)).wait_recv()
            return c2

        lax.fori_loop(0, n_col - 1, row_wait, 0)
        whole = log2_sum(rs_recv[...])
        t_ref[me_col] = t_ref[me_col] + (log2_a - whole[0])

        def row_send(s, c2):
            gather_copy(lax.rem(me_col + 1 + s, n_col), me_col).start()
            return c2

        lax.fori_loop(0, n_col - 1, row_send, 0)

        def col_step(s, c2):
            q = lax.rem(me_col + s, n_col)

            @pl.when(s > 0)
            def _():
                gather_copy(me_col, q).wait_recv()

            a_ref[q, pl.ds(3 * dim, slab), :] = with_bias(abase[q], t_ref[q], 0).astype(
                jnp.bfloat16
            )
            at_ref[q, :, pl.ds(depth // 2, depth // 2)] = a_ref[
                q, pl.ds(depth // 2, depth // 2), :
            ].T
            points = at_ref[q]
            for c in range(col_blocks):
                lanes = pl.ds(c * block, block)
                scores = jnp.dot(points, b_ref[:, lanes], preferred_element_type=jnp.float32)
                peak = jnp.max(scores, axis=0, keepdims=True)
                total = jnp.sum(jnp.exp2(scores - peak), axis=0, keepdims=True)
                lc_ref[q, :, lanes] = peak + jnp.log2(total)
            return c2

        lax.fori_loop(0, n_col, col_step, 0)
        c_send[k] = log2_sum(lc_ref[...])[0]

        def col_send(s, c2):
            col_copy(lax.rem(me_row + 1 + s, n_row), me_row, k).start()
            return c2

        lax.fori_loop(0, n_row - 1, col_send, 0)
        c_recv[k, me_row] = c_send[k]

        def row_done(s, c2):
            peer = lax.rem(me_col + 1 + s, n_col)
            scatter_copy(peer, me_col).wait_send()
            gather_copy(peer, me_col).wait_send()
            return c2

        lax.fori_loop(0, n_col - 1, row_done, 0)

        def col_wait(s, c2):
            col_copy(me_row, lax.rem(me_row + 1 + s, n_row), k).wait_recv()
            return c2

        lax.fori_loop(0, n_row - 1, col_wait, 0)
        u_ref[...] = u_ref[...] + (log2_b - log2_sum(c_recv[k])[0])
        b_ref[pl.ds(3 * dim, slab), :] = with_bias(bbase[...], u_ref[...], 3).astype(jnp.bfloat16)
        bt_ref[:, pl.ds(depth // 2, depth // 2)] = b_ref[pl.ds(depth // 2, depth // 2), :].T
        return carry

    lax.fori_loop(0, ITERS, iteration, 0)

    for q in range(n_col):
        potential = (t_ref[q] + nx_ref[q]) * (1.0 / kappa)
        for part in range(per):
            f_ref[pl.ds(q * per + part, 1), :] = potential[:, part * block : (part + 1) * block]
    potential = (u_ref[...] + ny_ref[...]) * (1.0 / kappa)
    for c in range(col_blocks):
        g_ref[pl.ds(c, 1), :] = potential[:, c * block : (c + 1) * block]

    def col_done(i, carry):
        peer = lax.rem(me_row + 1 + lax.rem(i, n_row - 1), n_row)
        col_copy(peer, me_row, i // (n_row - 1)).wait_send()
        return carry

    lax.fori_loop(0, ITERS * (n_row - 1), col_done, 0)


def body(n_row, n_col, row_points, col_points, block_lists):
    row_blocks, dim, block = row_points.shape
    col_blocks = col_points.shape[0]
    width = row_blocks // n_col * block
    cols = col_blocks * block
    f32, bf16 = jnp.float32, jnp.bfloat16
    pairs = row_blocks * col_blocks * block * block
    vmem = pl.BlockSpec(memory_space=pltpu.VMEM)
    return pl.pallas_call(
        functools.partial(kernel, n_row, n_col),
        out_shape=(
            jax.ShapeDtypeStruct((row_blocks, block), f32),
            jax.ShapeDtypeStruct((col_blocks, block), f32),
        ),
        in_specs=[vmem] * 3,
        out_specs=(vmem, vmem),
        scratch_shapes=[
            pltpu.VMEM((n_col, depth, width), bf16),
            pltpu.VMEM((n_col, width, depth), bf16),
            pltpu.VMEM((depth, cols), bf16),
            pltpu.VMEM((cols, depth), bf16),
            pltpu.VMEM((n_col, slab, width), f32),
            pltpu.VMEM((slab, cols), f32),
            pltpu.VMEM((n_col, 1, width), f32),
            pltpu.VMEM((1, cols), f32),
            pltpu.VMEM((n_col, 1, width), f32),
            pltpu.VMEM((1, cols), f32),
            pltpu.VMEM((n_col, 1, width), f32),
            pltpu.VMEM((n_col, 1, width), f32),
            pltpu.VMEM((n_col, 1, cols), f32),
            pltpu.VMEM((ITERS, 1, cols), f32),
            pltpu.VMEM((ITERS, n_row, 1, cols), f32),
            pltpu.VMEM((col_blocks, block, width), f32),
            pltpu.SemaphoreType.DMA((n_col,)),
            pltpu.SemaphoreType.DMA((n_col,)),
            pltpu.SemaphoreType.DMA((n_col,)),
            pltpu.SemaphoreType.DMA((n_col,)),
            pltpu.SemaphoreType.DMA((ITERS, n_row)),
            pltpu.SemaphoreType.DMA((ITERS, n_row)),
        ],
        compiler_params=pltpu.CompilerParams(
            collective_id=0, has_side_effects=True, vmem_limit_bytes=56 * 1024 * 1024
        ),
        cost_estimate=pl.CostEstimate(
            flops=2 * 2 * ITERS * pairs * depth,
            bytes_accessed=row_blocks * dim * block * 2,
            transcendentals=2 * ITERS * pairs,
        ),
    )(block_lists, row_points, col_points)


def solution(mesh):
    placed = (P("row", None, None), P("col", None, None), P("row", None))
    return jax.shard_map(
        functools.partial(body, mesh.shape["row"], mesh.shape["col"]),
        mesh=mesh,
        in_specs=placed,
        out_specs=(P("row", None), P("col", None)),
        check_vma=False,
    )
```

time: 731 us -> 88.7 us (0.12)
  blocking collectives: 318 us -> 0 us
  local copies, waits for them, and re-layouts: 283 us -> 1.92 us
  matrix products: 91.3 us -> 0 us
  Pallas kernels: 0 us -> 85.9 us
  other arithmetic: 26.6 us -> 0 us
    gather x274 -> x0, local copies, waits for them, and re-layouts: 280 us -> none  [the longest x64 103 us: tile_partials(): row_tiles = row_points[row_index]]
    pmax x8 -> x0, blocking collectives: 160 us -> none  [the longest x4 138 us: body(): whole_peak = lax.pmax(block_peak, 'col')]
    psum x8 -> x0, blocking collectives: 158 us -> none  [the longest x4 132 us: body(): whole_sum = lax.psum(block_sum * jnp.exp(block_peak - whole_peak), 'col')]
    dot_general x72 -> x0, matrix products: 91.3 us -> none  [the longest x64 89.7 us: tile_partials(): jnp.einsum('sdp,sdq->spq', row_tiles, col_tiles, preferred_element_type=j...]
    pallas_call x0 -> x1, Pallas kernels: none -> 85.9 us  [body(): pl.pallas_call(functools.partial(kernel, n_row, n_col), out_shape=(jax.Sh...]
    reduce_sum x67 -> x0, other arithmetic: 21.1 us -> none  [the longest x64 18.9 us: tile_partials(): jnp.sum(jnp.exp(scores - jnp.expand_dims(peak_vals, reduce_axis)), axis=r...]
where the time goes in v1:
time: 88.7 us; the launch traced here: 88.5 us
  Pallas kernels  85.9 us (97%)
  local copies, waits for them, and re-layouts  1.92 us (2%)
    pallas_call x1, Pallas kernels, body(): pl.pallas_call(functools.partial(kernel, n_row, n_col), out_shape=(jax.Sh...  85.9 us
    unnamed x4, local copies, waits for them, and re-layouts  1.92 us

profile of v1, /device:TPU:0, one launch (start us, length us, event | category | flops | bytes accessed | tf_op | source)
XLA Modules:
  0.0 88.5 jit_solution(15656006761205377165)
XLA Ops:
  0.6 85.9 %shard_map.50 = (f32[16,256]{1,0:T(8,128)}, f32[4,256]{1,0:T(4,128)}) custom-call(s32[16,16]{1,0:T(8,128)} %lists_ref.1, bf16[16,64,256]{2,1,0:T(8,128)(2,1)} %x_ref.1, bf16[4,64,256]{2,1,0:T(8,128)(2,1)} %y_ref.1), custom_call_target="tpu_custom_call" | custom-call | flops 17179869184 | bytes 524288 | tf_op jit(solution)/shard_map/pallas_call | solution.py:254
  86.5 0.0 copy-start
  86.5 1.3 %copy.7 = f32[16,256]{1,0:T(8,128)} copy(f32[16,256]{1,0:T(8,128)} %get-tuple-element.4) | data formatting | bytes 32768
  87.9 0.0 copy-done
  87.9 0.6 copy.8
Async XLA Ops:
  86.5 1.3 %copy-start = (f32[4,256]{1,0:T(4,128)S(1)}, f32[4,256]{1,0:T(4,128)}, u32[]{:S(2)}) copy-start(f32[4,256]{1,0:T(4,128)} %get-tuple-element.5) | copy-start | bytes 12292

commit v2 on v1

--- a/solution.py
+++ b/solution.py
@@ -12,6 +12,8 @@
 eps_reg = 0.05
 kappa = math.log2(math.e) / eps_reg
 masked_score = -(2.0**40)
+lift = 100.0
+least, most = 2.0**-80, 2.0**126
 depth = 256
 slab = 16
 MESH = pl.DeviceIdType.MESH
@@ -38,11 +40,16 @@
     return peak + jnp.log2(jnp.sum(jnp.exp2(parts - peak), axis=0, keepdims=True))
 
 
+def lifted_log2(total):
+    inside = (total > least) & (total < most)
+    return jnp.log2(jnp.where(inside, total, jnp.nan))
+
+
 def kernel(
-    n_row, n_col, lists_ref, x_ref, y_ref, f_ref, g_ref,
+    exact, n_row, n_col, lists_ref, x_ref, y_ref, f_ref, g_ref, flag_ref,
     a_ref, at_ref, b_ref, bt_ref, abase, bbase, t_ref, u_ref, nx_ref, ny_ref,
-    l_ref, rs_recv, lc_ref, c_send, c_recv, s_ref,
-    rs_ssem, rs_rsem, ag_ssem, ag_rsem, c_ssem, c_rsem,
+    l_ref, rs_recv, lc_ref, c_send, c_recv, s_ref, sums_ref, flag_recv,
+    rs_ssem, rs_rsem, ag_ssem, ag_rsem, c_ssem, c_rsem, flag_ssem, flag_rsem,
 ):
     me_row = lax.axis_index("row")
     me_col = lax.axis_index("col")
@@ -55,6 +62,7 @@
     log2_b = -math.log2(n_col * cols)
     alpha = 2.0 * kappa / dim
     beta = kappa / dim
+    raise_by = 0.0 if exact else lift
 
     barrier = pltpu.get_barrier_semaphore()
     for step in range(1, n_col):
@@ -102,7 +110,7 @@
                 fill = jnp.broadcast_to(jnp.where(hit > 0.0, 0.0, masked_score), (slab, block))
                 base = jnp.where(slab_rows == 6 + c, fill, base)
             abase[q, :, lanes] = base
-            a_ref[q, pl.ds(3 * dim, slab), lanes] = with_bias(base, -norm, 0).astype(jnp.bfloat16)
+            a_ref[q, pl.ds(3 * dim, slab), lanes] = with_bias(base, raise_by - norm, 0).astype(jnp.bfloat16)
             a_ref[q, pl.ds(3 * dim + slab, depth - 3 * dim - slab), lanes] = zeros
             at_ref[q, pl.ds(part * block, block), :] = a_ref[q, :, lanes].T
         return carry
@@ -112,6 +120,14 @@
 
     def row_part(q):
         points = a_ref[q]
+        if not exact:
+            total = jnp.zeros((8, width), jnp.float32)
+            for c in range(col_blocks):
+                scores = jnp.dot(
+                    bt_ref[pl.ds(c * block, block), :], points, preferred_element_type=jnp.float32
+                )
+                total += jnp.sum(jnp.exp2(scores).reshape(block // 8, 8, width), axis=0)
+            return jnp.sum(total, axis=0, keepdims=True)
         peak = None
         for c in range(col_blocks):
             scores = jnp.dot(
@@ -147,6 +163,11 @@
             device_id={"row": peer}, device_id_type=MESH,
         )
 
+    def combined(parts):
+        if exact:
+            return log2_sum(parts)[0]
+        return lifted_log2(jnp.sum(parts, axis=0))
+
     def iteration(k, carry):
         def row_step(s, c2):
             q = lax.rem(me_col + 1 + s, n_col)
@@ -166,8 +187,7 @@
             return c2
 
         lax.fori_loop(0, n_col - 1, row_wait, 0)
-        whole = log2_sum(rs_recv[...])
-        t_ref[me_col] = t_ref[me_col] + (log2_a - whole[0])
+        t_ref[me_col] = t_ref[me_col] + ((log2_a + raise_by) - combined(rs_recv[...]))
 
         def row_send(s, c2):
             gather_copy(lax.rem(me_col + 1 + s, n_col), me_col).start()
@@ -182,7 +202,7 @@
             def _():
                 gather_copy(me_col, q).wait_recv()
 
-            a_ref[q, pl.ds(3 * dim, slab), :] = with_bias(abase[q], t_ref[q], 0).astype(
+            a_ref[q, pl.ds(3 * dim, slab), :] = with_bias(abase[q], t_ref[q] + raise_by, 0).astype(
                 jnp.bfloat16
             )
             at_ref[q, :, pl.ds(depth // 2, depth // 2)] = a_ref[
@@ -192,13 +212,22 @@
             for c in range(col_blocks):
                 lanes = pl.ds(c * block, block)
                 scores = jnp.dot(points, b_ref[:, lanes], preferred_element_type=jnp.float32)
-                peak = jnp.max(scores, axis=0, keepdims=True)
-                total = jnp.sum(jnp.exp2(scores - peak), axis=0, keepdims=True)
-                lc_ref[q, :, lanes] = peak + jnp.log2(total)
-            return c2
-
+                if exact:
+                    peak = jnp.max(scores, axis=0, keepdims=True)
+                    total = jnp.sum(jnp.exp2(scores - peak), axis=0, keepdims=True)
+                    lc_ref[q, :, lanes] = peak + jnp.log2(total)
+                else:
+                    sums_ref[:, lanes] += jnp.sum(
+                        jnp.exp2(scores).reshape(width // 8, 8, block), axis=0
+                    )
+            return c2
+
+        sums_ref[...] = jnp.zeros((8, cols), jnp.float32)
         lax.fori_loop(0, n_col, col_step, 0)
-        c_send[k] = log2_sum(lc_ref[...])[0]
+        if exact:
+            c_send[k] = log2_sum(lc_ref[...])[0]
+        else:
+            c_send[k] = jnp.sum(sums_ref[...], axis=0, keepdims=True)
 
         def col_send(s, c2):
             col_copy(lax.rem(me_row + 1 + s, n_row), me_row, k).start()
@@ -220,12 +249,33 @@
             return c2
 
         lax.fori_loop(0, n_row - 1, col_wait, 0)
-        u_ref[...] = u_ref[...] + (log2_b - log2_sum(c_recv[k])[0])
+        u_ref[...] = u_ref[...] + ((log2_b + raise_by) - combined(c_recv[k]))
         b_ref[pl.ds(3 * dim, slab), :] = with_bias(bbase[...], u_ref[...], 3).astype(jnp.bfloat16)
         bt_ref[:, pl.ds(depth // 2, depth // 2)] = b_ref[pl.ds(depth // 2, depth // 2), :].T
         return carry
 
     lax.fori_loop(0, ITERS, iteration, 0)
+
+    def flag_copy(peer, slot):
+        return pltpu.make_async_remote_copy(
+            src_ref=flag_recv.at[slot], dst_ref=flag_recv.at[slot],
+            send_sem=flag_ssem.at[peer], recv_sem=flag_rsem.at[slot],
+            device_id={"col": peer}, device_id_type=MESH,
+        )
+
+    def flag_send(s, carry):
+        flag_copy(lax.rem(me_col + 1 + s, n_col), me_col).start()
+        return carry
+
+    def flag_wait(s, carry):
+        peer = lax.rem(me_col + 1 + s, n_col)
+        flag_copy(me_col, peer).wait_recv()
+        flag_copy(peer, me_col).wait_send()
+        return carry
+
+    if not exact:
+        flag_recv[me_col] = sum(u_ref[:, i * 128 : (i + 1) * 128] for i in range(cols // 128))
+        lax.fori_loop(0, n_col - 1, flag_send, 0)
 
     for q in range(n_col):
         potential = (t_ref[q] + nx_ref[q]) * (1.0 / kappa)
@@ -241,9 +291,15 @@
         return carry
 
     lax.fori_loop(0, ITERS * (n_row - 1), col_done, 0)
-
-
-def body(n_row, n_col, row_points, col_points, block_lists):
+    if exact:
+        flag_ref[...] = jnp.zeros_like(flag_ref)
+    else:
+        lax.fori_loop(0, n_col - 1, flag_wait, 0)
+        seen = jnp.sum(jnp.sum(flag_recv[...], axis=0), axis=1, keepdims=True)
+        flag_ref[...] = jnp.broadcast_to(jnp.where(seen == seen, 0, 1), flag_ref.shape)
+
+
+def run(exact, n_row, n_col, row_points, col_points, block_lists):
     row_blocks, dim, block = row_points.shape
     col_blocks = col_points.shape[0]
     width = row_blocks // n_col * block
@@ -252,13 +308,14 @@
     pairs = row_blocks * col_blocks * block * block
     vmem = pl.BlockSpec(memory_space=pltpu.VMEM)
     return pl.pallas_call(
-        functools.partial(kernel, n_row, n_col),
+        functools.partial(kernel, exact, n_row, n_col),
         out_shape=(
             jax.ShapeDtypeStruct((row_blocks, block), f32),
             jax.ShapeDtypeStruct((col_blocks, block), f32),
+            jax.ShapeDtypeStruct((1, 128), jnp.int32),
         ),
         in_specs=[vmem] * 3,
-        out_specs=(vmem, vmem),
+        out_specs=(vmem, vmem, vmem),
         scratch_shapes=[
             pltpu.VMEM((n_col, depth, width), bf16),
             pltpu.VMEM((n_col, width, depth), bf16),
@@ -275,16 +332,20 @@
             pltpu.VMEM((n_col, 1, cols), f32),
             pltpu.VMEM((ITERS, 1, cols), f32),
             pltpu.VMEM((ITERS, n_row, 1, cols), f32),
-            pltpu.VMEM((col_blocks, block, width), f32),
+            pltpu.VMEM((col_blocks, block, width) if exact else (1, 8, 128), f32),
+            pltpu.VMEM((8, cols), f32),
+            pltpu.VMEM((n_col, 1, 128), f32),
             pltpu.SemaphoreType.DMA((n_col,)),
             pltpu.SemaphoreType.DMA((n_col,)),
             pltpu.SemaphoreType.DMA((n_col,)),
             pltpu.SemaphoreType.DMA((n_col,)),
             pltpu.SemaphoreType.DMA((ITERS, n_row)),
             pltpu.SemaphoreType.DMA((ITERS, n_row)),
+            pltpu.SemaphoreType.DMA((n_col,)),
+            pltpu.SemaphoreType.DMA((n_col,)),
         ],
         compiler_params=pltpu.CompilerParams(
-            collective_id=0, has_side_effects=True, vmem_limit_bytes=56 * 1024 * 1024
+            collective_id=int(exact), has_side_effects=True, vmem_limit_bytes=56 * 1024 * 1024
         ),
         cost_estimate=pl.CostEstimate(
             flops=2 * 2 * ITERS * pairs * depth,
@@ -292,6 +353,18 @@
             transcendentals=2 * ITERS * pairs,
         ),
     )(block_lists, row_points, col_points)
+
+
+def body(n_row, n_col, *arguments):
+    row_potential, col_potential, flag = run(False, n_row, n_col, *arguments)
+    return lax.cond(
+        flag[0, 0] > 0,
+        lambda *operands: run(True, n_row, n_col, *operands[2:])[:2],
+        lambda *operands: operands[:2],
+        row_potential,
+        col_potential,
+        *arguments,
+    )
 
 
 def solution(mesh):

time: 88.7 us -> 158 us (1.78)
  Pallas kernels: 85.9 us -> 155 us
    pallas_call x1 -> x2, Pallas kernels: 85.9 us -> 155 us  [run(): pl.pallas_call(functools.partial(kernel, exact, n_row, n_col), out_shape=...]
where the time goes in v2:
time: 158 us
  Pallas kernels  155 us (98%)
    pallas_call x2, Pallas kernels, run(): pl.pallas_call(functools.partial(kernel, exact, n_row, n_col), out_shape=...  155 us

profile of v2, /device:TPU:0, one launch (start us, length us, event | category | flops | bytes accessed | tf_op | source)
XLA Modules:
  0.0 158.0 jit_solution(5378462974867942026)
XLA Ops:
  0.6 0.0 copy-start
  0.6 0.0 copy-start.1
  0.6 74.7 %shard_map.54 = (f32[16,256]{1,0:T(8,128)S(1)}, f32[4,256]{1,0:T(4,128)S(1)}, s32[1,128]{1,0:T(1,128)}) custom-call(s32[16,16]{1,0:T(8,128)} %lists_ref.1, bf16[16,64,256]{2,1,0:T(8,128)(2,1)} %x_ref.1, bf16[4,64,256]{2,1,0:T(8,128)(2,1)} %y_ref.1), custom_call_target="tpu_custom_call" | custom-call | flops 17179869184 | bytes 524288 | tf_op jit(solution)/shard_map/pallas_call | solution.py:310
  75.4 0.0 copy-start.2
  76.0 0.0 copy-done
  76.0 0.0 copy-done.1
  76.0 0.1 copy-done.2
  76.1 80.8 %conditional.1 = ((f32[16,256]{1,0:T(8,128)S(1)}, f32[4,256]{1,0:T(4,128)S(1)})) conditional(s32[]{:T(128)} %bitcast, (f32[16,256]{1,0:T(8,128)S(1)}, f32[4,256]{1,0:T(4,128)S(1)}) %tuple.14, (s32[16,16]{1,0:T(8,128)S(1)}, bf16[16,64,256]{2,1,0:T(8,128)(2,1)S(1)}, bf16[4,64,256]{2,1,0:T(8,128)(2,1)S(1)}) %tuple.28), branch_computations={%region_0.0_spmd, %region_1.0_spmd} | conditional | flops 17179869184 | bytes 524312 | solution.py:360
  76.1 80.8 %branch_1_fun.1 = (f32[16,256]{1,0:T(8,128)S(1)}, f32[4,256]{1,0:T(4,128)S(1)}, s32[1,128]{1,0:T(1,128)}) custom-call(s32[16,16]{1,0:T(8,128)S(1)} %get-tuple-element.10.lists_ref, bf16[16,64,256]{2,1,0:T(8,128)(2,1)S(1)} %get-tuple-element.11.x_ref, bf16[4,64,256]{2,1,0:T(8,128)(2,1)S(1)} %get-tuple-element.12.y_ref), custom_call_target="tpu_custom_call" | custom-call | flops 17179869184 | bytes 524288 | tf_op jit(solution)/shard_map/cond/branch_1_fun/pallas_call | solution.py:310
  156.8 0.6 copy.15
  157.4 0.6 copy.16
Async XLA Ops:
  0.6 75.3 %copy-start = (bf16[16,64,256]{2,1,0:T(8,128)(2,1)S(1)}, bf16[16,64,256]{2,1,0:T(8,128)(2,1)}, u32[]{:S(2)}) copy-start(bf16[16,64,256]{2,1,0:T(8,128)(2,1)} %x_ref.1) | copy-start | bytes 1572868
  0.6 75.3 %copy-start.1 = (bf16[4,64,256]{2,1,0:T(8,128)(2,1)S(1)}, bf16[4,64,256]{2,1,0:T(8,128)(2,1)}, u32[]{:S(2)}) copy-start(bf16[4,64,256]{2,1,0:T(8,128)(2,1)} %y_ref.1) | copy-start | bytes 393220
  75.4 0.7 copy-start.2

commit v3 on v2

--- a/solution.py
+++ b/solution.py
@@ -15,6 +15,7 @@
 lift = 100.0
 least, most = 2.0**-80, 2.0**126
 depth = 256
+group = 4
 slab = 16
 MESH = pl.DeviceIdType.MESH
 
@@ -355,8 +356,301 @@
     )(block_lists, row_points, col_points)
 
 
+def fast_kernel(
+    n_row, n_col, lists_ref, x_ref, y_ref, f_ref, g_ref, flag_ref,
+    a_ref, at_ref, b_ref, bt_ref, abase, bbase, t_ref, u_ref, nx_ref, ny_ref,
+    l_ref, rs_recv, c_send, c_recv, sums_ref, flag_recv,
+    rs_ssem, rs_rsem, ag_ssem, ag_rsem, c_ssem, c_rsem, flag_ssem, flag_rsem,
+):
+    me_row = lax.axis_index("row")
+    me_col = lax.axis_index("col")
+    row_blocks, dim, block = x_ref.shape
+    col_blocks = y_ref.shape[0]
+    per = row_blocks // n_col
+    part_width = per * block // 2
+    cols = col_blocks * block
+    half = cols // 2
+    log2_a = -math.log2(n_row * row_blocks * block)
+    log2_b = -math.log2(n_col * cols)
+    alpha = 2.0 * kappa / dim
+    beta = kappa / dim
+    bias_rows = pl.ds(3 * dim, slab)
+    spare_rows = pl.ds(3 * dim + slab, depth - 3 * dim - slab)
+    changing = pl.ds(depth // 2, depth // 2)
+
+    barrier = pltpu.get_barrier_semaphore()
+    for step in range(1, n_col):
+        pl.semaphore_signal(
+            barrier, inc=1, device_id={"col": lax.rem(me_col + step, n_col)}, device_id_type=MESH
+        )
+    for step in range(1, n_row):
+        pl.semaphore_signal(
+            barrier, inc=1, device_id={"row": lax.rem(me_row + step, n_row)}, device_id_type=MESH
+        )
+
+    slab_rows = lax.broadcasted_iota(jnp.int32, (slab, block), 0)
+    zeros = jnp.zeros((depth - 3 * dim - slab, block), jnp.bfloat16)
+
+    for c in range(col_blocks):
+        lanes = pl.ds(c * block, block)
+        y = y_ref[c]
+        for part in range(3):
+            b_ref[pl.ds(part * dim, dim), lanes] = y
+        y32 = y.astype(jnp.float32)
+        norm = jnp.sum(y32 * y32, axis=0, keepdims=True) * beta
+        ny_ref[:, lanes] = norm
+        u_ref[:, lanes] = -norm
+        base = jnp.where((slab_rows < 3) | (slab_rows == 6 + c), 1.0, 0.0)
+        bbase[:, lanes] = base
+        b_ref[bias_rows, lanes] = with_bias(base, -norm, 3).astype(jnp.bfloat16)
+        b_ref[spare_rows, lanes] = zeros
+        bt_ref[pl.ds(c * block, block), :] = b_ref[:, lanes].T
+
+    def prepare(q, carry):
+        for i in range(per):
+            r = q * per + i
+            lanes = pl.ds(i * block, block)
+            x = x_ref[r].astype(jnp.float32)
+            norm = jnp.sum(x * x, axis=0, keepdims=True) * beta
+            part, inner = divmod(i * block, part_width)
+            nx_ref[part, q, :, pl.ds(inner, block)] = norm
+            t_ref[part, q, :, pl.ds(inner, block)] = -norm
+            for j, piece in enumerate(split3(x * alpha)):
+                a_ref[q, pl.ds(j * dim, dim), lanes] = piece.astype(jnp.bfloat16)
+            listed = lists_ref[pl.ds(r, 1), :]
+            base = jnp.where((slab_rows >= 3) & (slab_rows < 6), 1.0, 0.0)
+            for c in range(col_blocks):
+                hit = jnp.where(listed == me_col * col_blocks + c, 1.0, 0.0)
+                hit = jnp.max(hit, axis=1, keepdims=True)
+                fill = jnp.broadcast_to(jnp.where(hit > 0.0, 0.0, masked_score), (slab, block))
+                base = jnp.where(slab_rows == 6 + c, fill, base)
+            abase[q, :, lanes] = base
+            a_ref[q, bias_rows, lanes] = with_bias(base, lift - norm, 0).astype(jnp.bfloat16)
+            a_ref[q, spare_rows, lanes] = zeros
+            at_ref[q, pl.ds(i * block, block), :] = a_ref[q, :, lanes].T
+        return carry
+
+    lax.fori_loop(0, n_col, prepare, 0)
+    pl.semaphore_wait(barrier, n_col - 1 + n_row - 1)
+
+    def scatter_copy(p, peer, slot):
+        return pltpu.make_async_remote_copy(
+            src_ref=l_ref.at[p, peer], dst_ref=rs_recv.at[p, slot],
+            send_sem=rs_ssem.at[p, peer], recv_sem=rs_rsem.at[p, slot],
+            device_id={"col": peer}, device_id_type=MESH,
+        )
+
+    def gather_copy(p, peer, slot):
+        return pltpu.make_async_remote_copy(
+            src_ref=t_ref.at[p, slot], dst_ref=t_ref.at[p, slot],
+            send_sem=ag_ssem.at[p, peer], recv_sem=ag_rsem.at[p, slot],
+            device_id={"col": peer}, device_id_type=MESH,
+        )
+
+    def col_copy(k, h, peer, slot):
+        return pltpu.make_async_remote_copy(
+            src_ref=c_send.at[k, h], dst_ref=c_recv.at[k, h, slot],
+            send_sem=c_ssem.at[k, h, peer], recv_sem=c_rsem.at[k, h, slot],
+            device_id={"row": peer}, device_id_type=MESH,
+        )
+
+    def flag_copy(peer, slot):
+        return pltpu.make_async_remote_copy(
+            src_ref=flag_recv.at[slot], dst_ref=flag_recv.at[slot],
+            send_sem=flag_ssem.at[peer], recv_sem=flag_rsem.at[slot],
+            device_id={"col": peer}, device_id_type=MESH,
+        )
+
+    col_peers = [lax.rem(me_col + step, n_col) for step in range(1, n_col)]
+    row_peers = [lax.rem(me_row + step, n_row) for step in range(1, n_row)]
+
+    def row_quarter(h, p):
+        def step(s, carry):
+            slices = [lax.rem(me_col + 1 + s * group + i, n_col) for i in range(group)]
+            totals = []
+            for q in slices:
+                scores = jnp.dot(
+                    bt_ref[pl.ds(h * half, half), :],
+                    a_ref[q, :, pl.ds(p * part_width, part_width)],
+                    preferred_element_type=jnp.float32,
+                )
+                total = jnp.sum(jnp.exp2(scores).reshape(half // 8, 8, part_width), axis=0)
+                totals.append(jnp.sum(total, axis=0, keepdims=True))
+            for i, q in enumerate(slices):
+                l_ref[p, q] = totals[i] if h == 0 else l_ref[p, q] + totals[i]
+            if h == 1:
+                for q in slices[:-1]:
+                    scatter_copy(p, q, me_col).start()
+
+                @pl.when(s < n_col // group - 1)
+                def _():
+                    scatter_copy(p, slices[-1], me_col).start()
+
+            return carry
+
+        lax.fori_loop(0, n_col // group, step, 0)
+
+    def col_quarter(h, p):
+        lanes = pl.ds(h * half, half)
+        points = pl.ds(p * part_width, part_width)
+
+        def step(s, total):
+            slices = [lax.rem(me_col + s * group + i, n_col) for i in range(group)]
+            if h == 0:
+                for q in slices:
+                    a_ref[q, bias_rows, points] = with_bias(
+                        abase[q, :, points], t_ref[p, q] + lift, 0
+                    ).astype(jnp.bfloat16)
+                    at_ref[q, points, changing] = a_ref[q, changing, points].T
+            for q in slices:
+                scores = jnp.dot(
+                    at_ref[q, points, :], b_ref[:, lanes], preferred_element_type=jnp.float32
+                )
+                total += jnp.sum(jnp.exp2(scores).reshape(part_width // 8, 8, half), axis=0)
+            return total
+
+        start = jnp.zeros((8, half), jnp.float32) if p == 0 else sums_ref[:, lanes]
+        total = lax.fori_loop(0, n_col // group, step, start)
+        if p == 0:
+            sums_ref[:, lanes] = total
+        return total
+
+    def gather(p):
+        rs_recv[p, me_col] = l_ref[p, me_col]
+        for peer in col_peers:
+            scatter_copy(p, me_col, peer).wait_recv()
+        whole = jnp.sum(rs_recv[p], axis=0)
+        t_ref[p, me_col] = t_ref[p, me_col] + ((log2_a + lift) - lifted_log2(whole))
+        for peer in col_peers:
+            gather_copy(p, peer, me_col).start()
+
+    def gathered(p):
+        for peer in col_peers:
+            gather_copy(p, me_col, peer).wait_recv()
+
+    def col_exchange(k, h, total):
+        total = jnp.sum(total, axis=0, keepdims=True)
+        c_send[k, h] = total
+        for peer in row_peers:
+            col_copy(k, h, peer, me_row).start()
+        c_recv[k, h, me_row] = total
+
+    def col_update(k, h, last):
+        lanes = pl.ds(h * half, half)
+        for peer in row_peers:
+            col_copy(k, h, me_row, peer).wait_recv()
+        whole = jnp.sum(c_recv[k, h], axis=0)
+        u_ref[:, lanes] = u_ref[:, lanes] + ((log2_b + lift) - lifted_log2(whole))
+        if not last:
+            b_ref[bias_rows, lanes] = with_bias(bbase[:, lanes], u_ref[:, lanes], 3).astype(
+                jnp.bfloat16
+            )
+            bt_ref[lanes, changing] = b_ref[changing, lanes].T
+
+    def iteration(k, carry):
+        for h in range(2):
+
+            @pl.when(k > 0)
+            def _():
+                col_update(k - 1, h, False)
+
+            row_quarter(h, 0)
+        row_quarter(0, 1)
+        gather(0)
+        row_quarter(1, 1)
+        gathered(0)
+        col_quarter(0, 0)
+        gather(1)
+        col_quarter(1, 0)
+        gathered(1)
+        col_exchange(k, 0, col_quarter(0, 1))
+        col_exchange(k, 1, col_quarter(1, 1))
+        for p in range(2):
+            for peer in col_peers:
+                scatter_copy(p, peer, me_col).wait_send()
+                gather_copy(p, peer, me_col).wait_send()
+        return carry
+
+    lax.fori_loop(0, ITERS, iteration, 0)
+
+    for q in range(n_col):
+        for i in range(per):
+            part, inner = divmod(i * block, part_width)
+            inner = pl.ds(inner, block)
+            f_ref[pl.ds(q * per + i, 1), :] = (
+                t_ref[part, q, :, inner] + nx_ref[part, q, :, inner]
+            ) * (1.0 / kappa)
+    for h in range(2):
+        col_update(ITERS - 1, h, True)
+    flag_recv[me_col] = sum(u_ref[:, i * 128 : (i + 1) * 128] for i in range(cols // 128))
+    for peer in col_peers:
+        flag_copy(peer, me_col).start()
+    potential = (u_ref[...] + ny_ref[...]) * (1.0 / kappa)
+    for c in range(col_blocks):
+        g_ref[pl.ds(c, 1), :] = potential[:, c * block : (c + 1) * block]
+    for k in range(ITERS):
+        for h in range(2):
+            for peer in row_peers:
+                col_copy(k, h, peer, me_row).wait_send()
+    for peer in col_peers:
+        flag_copy(me_col, peer).wait_recv()
+        flag_copy(peer, me_col).wait_send()
+    seen = jnp.sum(jnp.sum(flag_recv[...], axis=0), axis=1, keepdims=True)
+    flag_ref[...] = jnp.broadcast_to(jnp.where(seen == seen, 0, 1), flag_ref.shape)
+
+
+def run_fast(n_row, n_col, row_points, col_points, block_lists):
+    row_blocks, dim, block = row_points.shape
+    col_blocks = col_points.shape[0]
+    width = row_blocks // n_col * block
+    cols = col_blocks * block
+    f32, bf16 = jnp.float32, jnp.bfloat16
+    pairs = row_blocks * col_blocks * block * block
+    vmem = pl.BlockSpec(memory_space=pltpu.VMEM)
+    sems = pltpu.SemaphoreType.DMA
+    return pl.pallas_call(
+        functools.partial(fast_kernel, n_row, n_col),
+        out_shape=(
+            jax.ShapeDtypeStruct((row_blocks, block), f32),
+            jax.ShapeDtypeStruct((col_blocks, block), f32),
+            jax.ShapeDtypeStruct((1, 128), jnp.int32),
+        ),
+        in_specs=[vmem] * 3,
+        out_specs=(vmem, vmem, vmem),
+        scratch_shapes=[
+            pltpu.VMEM((n_col, depth, width), bf16),
+            pltpu.VMEM((n_col, width, depth), bf16),
+            pltpu.VMEM((depth, cols), bf16),
+            pltpu.VMEM((cols, depth), bf16),
+            pltpu.VMEM((n_col, slab, width), f32),
+            pltpu.VMEM((slab, cols), f32),
+            pltpu.VMEM((2, n_col, 1, width // 2), f32),
+            pltpu.VMEM((1, cols), f32),
+            pltpu.VMEM((2, n_col, 1, width // 2), f32),
+            pltpu.VMEM((1, cols), f32),
+            pltpu.VMEM((2, n_col, 1, width // 2), f32),
+            pltpu.VMEM((2, n_col, 1, width // 2), f32),
+            pltpu.VMEM((ITERS, 2, 1, cols // 2), f32),
+            pltpu.VMEM((ITERS, 2, n_row, 1, cols // 2), f32),
+            pltpu.VMEM((8, cols), f32),
+            pltpu.VMEM((n_col, 1, 128), f32),
+            sems((2, n_col)), sems((2, n_col)), sems((2, n_col)), sems((2, n_col)),
+            sems((ITERS, 2, n_row)), sems((ITERS, 2, n_row)),
+            sems((n_col,)), sems((n_col,)),
+        ],
+        compiler_params=pltpu.CompilerParams(
+            collective_id=0, has_side_effects=True, vmem_limit_bytes=40 * 1024 * 1024
+        ),
+        cost_estimate=pl.CostEstimate(
+            flops=2 * 2 * ITERS * pairs * depth,
+            bytes_accessed=row_blocks * dim * block * 2,
+            transcendentals=2 * ITERS * pairs,
+        ),
+    )(block_lists, row_points, col_points)
+
+
 def body(n_row, n_col, *arguments):
-    row_potential, col_potential, flag = run(False, n_row, n_col, *arguments)
+    row_potential, col_potential, flag = run_fast(n_row, n_col, *arguments)
     return lax.cond(
         flag[0, 0] > 0,
         lambda *operands: run(True, n_row, n_col, *operands[2:])[:2],

time: 158 us -> 171 us (1.082)
  Pallas kernels: 155 us -> 168 us
    pallas_call x0 -> x1, Pallas kernels: none -> 86.4 us  [run_fast(): pl.pallas_call(functools.partial(fast_kernel, n_row, n_col), out_shape=(j...]
    pallas_call x2 -> x1, Pallas kernels: 155 us -> 82.1 us  [run(): pl.pallas_call(functools.partial(kernel, exact, n_row, n_col), out_shape=...]
where the time goes in v3:
time: 171 us
  Pallas kernels  168 us (98%)
  local copies, waits for them, and re-layouts  1.84 us (1%)
    pallas_call x1, Pallas kernels, run_fast(): pl.pallas_call(functools.partial(fast_kernel, n_row, n_col), out_shape=(j...  86.4 us
    pallas_call x1, Pallas kernels, run(): pl.pallas_call(functools.partial(kernel, exact, n_row, n_col), out_shape=...  82.1 us

profile of v3, /device:TPU:0, one launch (start us, length us, event | category | flops | bytes accessed | tf_op | source)
XLA Modules:
  0.0 171.1 jit_solution(15340377597517911087)
XLA Ops:
  0.6 0.0 copy-start
  0.6 0.0 copy-start.1
  0.6 86.4 %shard_map.54 = (f32[16,256]{1,0:T(8,128)S(1)}, f32[4,256]{1,0:T(4,128)S(1)}, s32[1,128]{1,0:T(1,128)S(1)}) custom-call(s32[16,16]{1,0:T(8,128)} %lists_ref.1, bf16[16,64,256]{2,1,0:T(8,128)(2,1)} %x_ref.1, bf16[4,64,256]{2,1,0:T(8,128)(2,1)} %y_ref.1), custom_call_target="tpu_custom_call" | custom-call | flops 17179869184 | bytes 524288 | tf_op jit(solution)/shard_map/pallas_call | solution.py:611
  87.1 0.0 copy-start.2
  87.1 0.0 copy-done
  87.1 0.0 copy-done.1
  87.1 0.6 copy-done.2
  87.8 82.1 %conditional.1 = ((f32[16,256]{1,0:T(8,128)S(1)}, f32[4,256]{1,0:T(4,128)S(1)})) conditional(s32[]{:T(128)} %bitcast, (f32[16,256]{1,0:T(8,128)S(1)}, f32[4,256]{1,0:T(4,128)S(1)}) %tuple.14, (s32[16,16]{1,0:T(8,128)S(1)}, bf16[16,64,256]{2,1,0:T(8,128)(2,1)S(1)}, bf16[4,64,256]{2,1,0:T(8,128)(2,1)S(1)}) %tuple.28), branch_computations={%region_0.0_spmd, %region_1.0_spmd} | conditional | flops 17179869184 | bytes 524312 | solution.py:654
  87.8 82.1 %branch_1_fun.1 = (f32[16,256]{1,0:T(8,128)S(1)}, f32[4,256]{1,0:T(4,128)S(1)}, s32[1,128]{1,0:T(1,128)}) custom-call(s32[16,16]{1,0:T(8,128)S(1)} %get-tuple-element.10.lists_ref, bf16[16,64,256]{2,1,0:T(8,128)(2,1)S(1)} %get-tuple-element.11.x_ref, bf16[4,64,256]{2,1,0:T(8,128)(2,1)S(1)} %get-tuple-element.12.y_ref), custom_call_target="tpu_custom_call" | custom-call | flops 17179869184 | bytes 524288 | tf_op jit(solution)/shard_map/cond/branch_1_fun/pallas_call | solution.py:311
  169.8 0.6 copy.15
  170.5 0.6 copy.16
Async XLA Ops:
  0.6 86.5 %copy-start = (bf16[16,64,256]{2,1,0:T(8,128)(2,1)S(1)}, bf16[16,64,256]{2,1,0:T(8,128)(2,1)}, u32[]{:S(2)}) copy-start(bf16[16,64,256]{2,1,0:T(8,128)(2,1)} %x_ref.1) | copy-start | bytes 1572868
  0.6 86.5 %copy-start.1 = (bf16[4,64,256]{2,1,0:T(8,128)(2,1)S(1)}, bf16[4,64,256]{2,1,0:T(8,128)(2,1)}, u32[]{:S(2)}) copy-start(bf16[4,64,256]{2,1,0:T(8,128)(2,1)} %y_ref.1) | copy-start | bytes 393220
  87.1 0.7 copy-start.2

commit v4 on v2

--- a/solution.py
+++ b/solution.py
@@ -355,8 +355,244 @@
     )(block_lists, row_points, col_points)
 
 
+def fast_kernel(
+    n_row, n_col, lists_ref, x_ref, y_ref, f_ref, g_ref, flag_ref,
+    a_ref, b_ref, bt_ref, abase, bbase, t_ref, u_ref, nx_ref, ny_ref,
+    l_ref, rs_recv, c_send, c_recv, sums_ref, flag_recv,
+    rs_ssem, rs_rsem, ag_ssem, ag_rsem, c_ssem, c_rsem, flag_ssem, flag_rsem,
+):
+    me_row = lax.axis_index("row")
+    me_col = lax.axis_index("col")
+    row_blocks, dim, block = x_ref.shape
+    col_blocks = y_ref.shape[0]
+    per = row_blocks // n_col
+    width = per * block
+    cols = col_blocks * block
+    log2_a = -math.log2(n_row * row_blocks * block)
+    log2_b = -math.log2(n_col * cols)
+    alpha = 2.0 * kappa / dim
+    beta = kappa / dim
+    bias_rows = pl.ds(3 * dim, slab)
+    spare_rows = pl.ds(3 * dim + slab, depth - 3 * dim - slab)
+    changing = pl.ds(depth // 2, depth // 2)
+
+    barrier = pltpu.get_barrier_semaphore()
+    for step in range(1, n_col):
+        pl.semaphore_signal(
+            barrier, inc=1, device_id={"col": lax.rem(me_col + step, n_col)}, device_id_type=MESH
+        )
+    for step in range(1, n_row):
+        pl.semaphore_signal(
+            barrier, inc=1, device_id={"row": lax.rem(me_row + step, n_row)}, device_id_type=MESH
+        )
+
+    slab_rows = lax.broadcasted_iota(jnp.int32, (slab, block), 0)
+    zeros = jnp.zeros((depth - 3 * dim - slab, block), jnp.bfloat16)
+
+    for c in range(col_blocks):
+        lanes = pl.ds(c * block, block)
+        y = y_ref[c]
+        for part in range(3):
+            b_ref[pl.ds(part * dim, dim), lanes] = y
+        y32 = y.astype(jnp.float32)
+        norm = jnp.sum(y32 * y32, axis=0, keepdims=True) * beta
+        ny_ref[:, lanes] = norm
+        u_ref[:, lanes] = -norm
+        base = jnp.where((slab_rows < 3) | (slab_rows == 6 + c), 1.0, 0.0)
+        bbase[:, lanes] = base
+        b_ref[bias_rows, lanes] = with_bias(base, -norm, 3).astype(jnp.bfloat16)
+        b_ref[spare_rows, lanes] = zeros
+        bt_ref[pl.ds(c * block, block), :] = b_ref[:, lanes].T
+
+    def prepare(q, carry):
+        for i in range(per):
+            r = q * per + i
+            lanes = pl.ds(i * block, block)
+            x = x_ref[r].astype(jnp.float32)
+            norm = jnp.sum(x * x, axis=0, keepdims=True) * beta
+            nx_ref[q, :, lanes] = norm
+            t_ref[q, :, lanes] = -norm
+            for j, piece in enumerate(split3(x * alpha)):
+                a_ref[q, pl.ds(j * dim, dim), lanes] = piece.astype(jnp.bfloat16)
+            listed = lists_ref[pl.ds(r, 1), :]
+            base = jnp.where((slab_rows >= 3) & (slab_rows < 6), 1.0, 0.0)
+            for c in range(col_blocks):
+                hit = jnp.where(listed == me_col * col_blocks + c, 1.0, 0.0)
+                hit = jnp.max(hit, axis=1, keepdims=True)
+                fill = jnp.broadcast_to(jnp.where(hit > 0.0, 0.0, masked_score), (slab, block))
+                base = jnp.where(slab_rows == 6 + c, fill, base)
+            abase[q, :, lanes] = base
+            a_ref[q, bias_rows, lanes] = with_bias(base, lift - norm, 0).astype(jnp.bfloat16)
+            a_ref[q, spare_rows, lanes] = zeros
+        return carry
+
+    lax.fori_loop(0, n_col, prepare, 0)
+    pl.semaphore_wait(barrier, n_col - 1 + n_row - 1)
+
+    def scatter_copy(peer):
+        return pltpu.make_async_remote_copy(
+            src_ref=l_ref.at[peer], dst_ref=rs_recv.at[me_col],
+            send_sem=rs_ssem, recv_sem=rs_rsem,
+            device_id={"col": peer}, device_id_type=MESH,
+        )
+
+    def gather_copy(peer):
+        return pltpu.make_async_remote_copy(
+            src_ref=t_ref.at[me_col], dst_ref=t_ref.at[me_col],
+            send_sem=ag_ssem, recv_sem=ag_rsem,
+            device_id={"col": peer}, device_id_type=MESH,
+        )
+
+    def col_copy(k, peer):
+        return pltpu.make_async_remote_copy(
+            src_ref=c_send.at[k], dst_ref=c_recv.at[k, me_row],
+            send_sem=c_ssem.at[k], recv_sem=c_rsem.at[k],
+            device_id={"row": peer}, device_id_type=MESH,
+        )
+
+    def flag_copy(peer):
+        return pltpu.make_async_remote_copy(
+            src_ref=flag_recv.at[me_col], dst_ref=flag_recv.at[me_col],
+            send_sem=flag_ssem, recv_sem=flag_rsem,
+            device_id={"col": peer}, device_id_type=MESH,
+        )
+
+    def wait_all(ref, peers, sem):
+        some = ref.at[pl.ds(0, peers)]
+        pltpu.make_async_copy(some, some, sem).wait()
+
+    col_peers = [lax.rem(me_col + step, n_col) for step in range(1, n_col)]
+    row_peers = [lax.rem(me_row + step, n_row) for step in range(1, n_row)]
+
+    def exponentials(q, i):
+        scores = jnp.dot(
+            bt_ref[...], a_ref[q, :, pl.ds(i * block, block)], preferred_element_type=jnp.float32
+        )
+        return jnp.exp2(scores)
+
+    def row_part(q):
+        for i in range(per):
+            total = jnp.sum(exponentials(q, i).reshape(cols // 8, 8, block), axis=0)
+            l_ref[q, :, pl.ds(i * block, block)] = jnp.sum(total, axis=0, keepdims=True)
+
+    def col_part(q):
+        a_ref[q, bias_rows, :] = with_bias(abase[q], t_ref[q] + lift, 0).astype(jnp.bfloat16)
+        for i in range(per):
+            terms = exponentials(q, i)
+            sums_ref[...] += sum(terms[:, j : j + 128] for j in range(0, block, 128))
+
+    def iteration(k, carry):
+        def row_step(s, c2):
+            q = lax.rem(me_col + 1 + s, n_col)
+            row_part(q)
+            scatter_copy(q).start()
+            return c2
+
+        lax.fori_loop(0, n_col - 1, row_step, 0)
+        row_part(me_col)
+        rs_recv[me_col] = l_ref[me_col]
+        wait_all(rs_recv, n_col - 1, rs_rsem)
+        whole = jnp.sum(rs_recv[...], axis=0)
+        t_ref[me_col] = t_ref[me_col] + ((log2_a + lift) - lifted_log2(whole))
+        for peer in col_peers:
+            gather_copy(peer).start()
+
+        sums_ref[...] = jnp.zeros((cols, 128), jnp.float32)
+        col_part(me_col)
+        wait_all(t_ref, n_col - 1, ag_rsem)
+
+        def col_step(s, c2):
+            col_part(lax.rem(me_col + 1 + s, n_col))
+            return c2
+
+        lax.fori_loop(0, n_col - 1, col_step, 0)
+        share = jnp.sum(sums_ref[...].T, axis=0, keepdims=True)
+        c_send[k] = share
+        for peer in row_peers:
+            col_copy(k, peer).start()
+        c_recv[k, me_row] = share
+        wait_all(l_ref, n_col - 1, rs_ssem)
+        wait_all(t_ref, n_col - 1, ag_ssem)
+        wait_all(c_recv.at[k], n_row - 1, c_rsem.at[k])
+        whole = jnp.sum(c_recv[k], axis=0)
+        u_ref[...] = u_ref[...] + ((log2_b + lift) - lifted_log2(whole))
+        b_ref[bias_rows, :] = with_bias(bbase[...], u_ref[...], 3).astype(jnp.bfloat16)
+        bt_ref[:, changing] = b_ref[changing, :].T
+        return carry
+
+    lax.fori_loop(0, ITERS, iteration, 0)
+
+    for q in range(n_col):
+        for i in range(per):
+            lanes = pl.ds(i * block, block)
+            f_ref[pl.ds(q * per + i, 1), :] = (t_ref[q, :, lanes] + nx_ref[q, :, lanes]) * (
+                1.0 / kappa
+            )
+    flag_recv[me_col] = sum(u_ref[:, i * 128 : (i + 1) * 128] for i in range(cols // 128))
+    for peer in col_peers:
+        flag_copy(peer).start()
+    potential = (u_ref[...] + ny_ref[...]) * (1.0 / kappa)
+    for c in range(col_blocks):
+        g_ref[pl.ds(c, 1), :] = potential[:, c * block : (c + 1) * block]
+    for k in range(ITERS):
+        wait_all(c_recv.at[k], n_row - 1, c_ssem.at[k])
+    wait_all(flag_recv, n_col - 1, flag_rsem)
+    wait_all(flag_recv, n_col - 1, flag_ssem)
+    seen = jnp.sum(jnp.sum(flag_recv[...], axis=0), axis=1, keepdims=True)
+    flag_ref[...] = jnp.broadcast_to(jnp.where(seen == seen, 0, 1), flag_ref.shape)
+
+
+def run_fast(n_row, n_col, row_points, col_points, block_lists):
+    row_blocks, dim, block = row_points.shape
+    col_blocks = col_points.shape[0]
+    width = row_blocks // n_col * block
+    cols = col_blocks * block
+    f32, bf16 = jnp.float32, jnp.bfloat16
+    pairs = row_blocks * col_blocks * block * block
+    vmem = pl.BlockSpec(memory_space=pltpu.VMEM)
+    sems = pltpu.SemaphoreType.DMA
+    return pl.pallas_call(
+        functools.partial(fast_kernel, n_row, n_col),
+        out_shape=(
+            jax.ShapeDtypeStruct((row_blocks, block), f32),
+            jax.ShapeDtypeStruct((col_blocks, block), f32),
+            jax.ShapeDtypeStruct((1, 128), jnp.int32),
+        ),
+        in_specs=[vmem] * 3,
+        out_specs=(vmem, vmem, vmem),
+        scratch_shapes=[
+            pltpu.VMEM((n_col, depth, width), bf16),
+            pltpu.VMEM((depth, cols), bf16),
+            pltpu.VMEM((cols, depth), bf16),
+            pltpu.VMEM((n_col, slab, width), f32),
+            pltpu.VMEM((slab, cols), f32),
+            pltpu.VMEM((n_col, 1, width), f32),
+            pltpu.VMEM((1, cols), f32),
+            pltpu.VMEM((n_col, 1, width), f32),
+            pltpu.VMEM((1, cols), f32),
+            pltpu.VMEM((n_col, 1, width), f32),
+            pltpu.VMEM((n_col, 1, width), f32),
+            pltpu.VMEM((ITERS, 1, cols), f32),
+            pltpu.VMEM((ITERS, n_row, 1, cols), f32),
+            pltpu.VMEM((cols, 128), f32),
+            pltpu.VMEM((n_col, 1, 128), f32),
+            sems, sems, sems, sems,
+            sems((ITERS,)), sems((ITERS,)),
+            sems, sems,
+        ],
+        compiler_params=pltpu.CompilerParams(
+            collective_id=0, has_side_effects=True, vmem_limit_bytes=40 * 1024 * 1024
+        ),
+        cost_estimate=pl.CostEstimate(
+            flops=2 * 2 * ITERS * pairs * depth,
+            bytes_accessed=row_blocks * dim * block * 2,
+            transcendentals=2 * ITERS * pairs,
+        ),
+    )(block_lists, row_points, col_points)
+
+
 def body(n_row, n_col, *arguments):
-    row_potential, col_potential, flag = run(False, n_row, n_col, *arguments)
+    row_potential, col_potential, flag = run_fast(n_row, n_col, *arguments)
     return lax.cond(
         flag[0, 0] > 0,
         lambda *operands: run(True, n_row, n_col, *operands[2:])[:2],

time: 158 us -> 164 us (1.038)
  Pallas kernels: 155 us -> 161 us
    pallas_call x0 -> x1, Pallas kernels: none -> 78.1 us  [run_fast(): pl.pallas_call(functools.partial(fast_kernel, n_row, n_col), out_shape=(j...]
    pallas_call x2 -> x1, Pallas kernels: 155 us -> 82.9 us  [run(): pl.pallas_call(functools.partial(kernel, exact, n_row, n_col), out_shape=...]
where the time goes in v4:
time: 164 us
  Pallas kernels  161 us (98%)
  local copies, waits for them, and re-layouts  1.84 us (1%)
    pallas_call x1, Pallas kernels, run(): pl.pallas_call(functools.partial(kernel, exact, n_row, n_col), out_shape=...  82.9 us
    pallas_call x1, Pallas kernels, run_fast(): pl.pallas_call(functools.partial(fast_kernel, n_row, n_col), out_shape=(j...  78.1 us

profile of v4, /device:TPU:0, one launch (start us, length us, event | category | flops | bytes accessed | tf_op | source)
XLA Modules:
  0.0 163.6 jit_solution(5311357759692437553)
XLA Ops:
  0.6 0.0 copy-start
  0.6 0.0 copy-start.1
  0.6 78.1 %shard_map.54 = (f32[16,256]{1,0:T(8,128)S(1)}, f32[4,256]{1,0:T(4,128)S(1)}, s32[1,128]{1,0:T(1,128)S(1)}) custom-call(s32[16,16]{1,0:T(8,128)} %lists_ref.1, bf16[16,64,256]{2,1,0:T(8,128)(2,1)} %x_ref.1, bf16[4,64,256]{2,1,0:T(8,128)(2,1)} %y_ref.1), custom_call_target="tpu_custom_call" | custom-call | flops 17179869184 | bytes 524288 | tf_op jit(solution)/shard_map/pallas_call | solution.py:554
  78.8 0.0 copy-start.2
  78.9 0.0 copy-done
  78.9 0.0 copy-done.1
  78.9 0.6 copy-done.2
  79.5 82.9 %conditional.1 = ((f32[16,256]{1,0:T(8,128)S(1)}, f32[4,256]{1,0:T(4,128)S(1)})) conditional(s32[]{:T(128)} %bitcast, (f32[16,256]{1,0:T(8,128)S(1)}, f32[4,256]{1,0:T(4,128)S(1)}) %tuple.14, (s32[16,16]{1,0:T(8,128)S(1)}, bf16[16,64,256]{2,1,0:T(8,128)(2,1)S(1)}, bf16[4,64,256]{2,1,0:T(8,128)(2,1)S(1)}) %tuple.28), branch_computations={%region_0.0_spmd, %region_1.0_spmd} | conditional | flops 17179869184 | bytes 524312 | solution.py:596
  79.5 82.9 %branch_1_fun.1 = (f32[16,256]{1,0:T(8,128)S(1)}, f32[4,256]{1,0:T(4,128)S(1)}, s32[1,128]{1,0:T(1,128)}) custom-call(s32[16,16]{1,0:T(8,128)S(1)} %get-tuple-element.10.lists_ref, bf16[16,64,256]{2,1,0:T(8,128)(2,1)S(1)} %get-tuple-element.11.x_ref, bf16[4,64,256]{2,1,0:T(8,128)(2,1)S(1)} %get-tuple-element.12.y_ref), custom_call_target="tpu_custom_call" | custom-call | flops 17179869184 | bytes 524288 | tf_op jit(solution)/shard_map/cond/branch_1_fun/pallas_call | solution.py:310
  162.4 0.6 copy.15
  163.0 0.6 copy.16
Async XLA Ops:
  0.6 78.2 %copy-start = (bf16[16,64,256]{2,1,0:T(8,128)(2,1)S(1)}, bf16[16,64,256]{2,1,0:T(8,128)(2,1)}, u32[]{:S(2)}) copy-start(bf16[16,64,256]{2,1,0:T(8,128)(2,1)} %x_ref.1) | copy-start | bytes 1572868
  0.6 78.2 %copy-start.1 = (bf16[4,64,256]{2,1,0:T(8,128)(2,1)S(1)}, bf16[4,64,256]{2,1,0:T(8,128)(2,1)}, u32[]{:S(2)}) copy-start(bf16[4,64,256]{2,1,0:T(8,128)(2,1)} %y_ref.1) | copy-start | bytes 393220
  78.8 0.7 copy-start.2

commit v5 on v4

--- a/solution.py
+++ b/solution.py
@@ -15,6 +15,7 @@
 lift = 100.0
 least, most = 2.0**-80, 2.0**126
 depth = 256
+shallow = 128
 slab = 16
 MESH = pl.DeviceIdType.MESH
 
@@ -372,9 +373,9 @@
     log2_b = -math.log2(n_col * cols)
     alpha = 2.0 * kappa / dim
     beta = kappa / dim
-    bias_rows = pl.ds(3 * dim, slab)
-    spare_rows = pl.ds(3 * dim + slab, depth - 3 * dim - slab)
-    changing = pl.ds(depth // 2, depth // 2)
+    bias_rows = pl.ds(dim, slab)
+    spare_rows = pl.ds(dim + slab, shallow - dim - slab)
+    inverse = 1.0 / alpha
 
     barrier = pltpu.get_barrier_semaphore()
     for step in range(1, n_col):
@@ -387,20 +388,19 @@
         )
 
     slab_rows = lax.broadcasted_iota(jnp.int32, (slab, block), 0)
-    zeros = jnp.zeros((depth - 3 * dim - slab, block), jnp.bfloat16)
+    zeros = jnp.zeros((shallow - dim - slab, block), jnp.bfloat16)
 
     for c in range(col_blocks):
         lanes = pl.ds(c * block, block)
         y = y_ref[c]
-        for part in range(3):
-            b_ref[pl.ds(part * dim, dim), lanes] = y
+        b_ref[pl.ds(0, dim), lanes] = y
         y32 = y.astype(jnp.float32)
         norm = jnp.sum(y32 * y32, axis=0, keepdims=True) * beta
         ny_ref[:, lanes] = norm
         u_ref[:, lanes] = -norm
         base = jnp.where((slab_rows < 3) | (slab_rows == 6 + c), 1.0, 0.0)
         bbase[:, lanes] = base
-        b_ref[bias_rows, lanes] = with_bias(base, -norm, 3).astype(jnp.bfloat16)
+        b_ref[bias_rows, lanes] = with_bias(base, norm * -inverse, 3).astype(jnp.bfloat16)
         b_ref[spare_rows, lanes] = zeros
         bt_ref[pl.ds(c * block, block), :] = b_ref[:, lanes].T
 
@@ -412,8 +412,7 @@
             norm = jnp.sum(x * x, axis=0, keepdims=True) * beta
             nx_ref[q, :, lanes] = norm
             t_ref[q, :, lanes] = -norm
-            for j, piece in enumerate(split3(x * alpha)):
-                a_ref[q, pl.ds(j * dim, dim), lanes] = piece.astype(jnp.bfloat16)
+            a_ref[q, pl.ds(0, dim), lanes] = x_ref[r]
             listed = lists_ref[pl.ds(r, 1), :]
             base = jnp.where((slab_rows >= 3) & (slab_rows < 6), 1.0, 0.0)
             for c in range(col_blocks):
@@ -422,7 +421,7 @@
                 fill = jnp.broadcast_to(jnp.where(hit > 0.0, 0.0, masked_score), (slab, block))
                 base = jnp.where(slab_rows == 6 + c, fill, base)
             abase[q, :, lanes] = base
-            a_ref[q, bias_rows, lanes] = with_bias(base, lift - norm, 0).astype(jnp.bfloat16)
+            a_ref[q, bias_rows, lanes] = with_bias(base, (lift - norm) * inverse, 0).astype(jnp.bfloat16)
             a_ref[q, spare_rows, lanes] = zeros
         return carry
 
@@ -464,22 +463,32 @@
     col_peers = [lax.rem(me_col + step, n_col) for step in range(1, n_col)]
     row_peers = [lax.rem(me_row + step, n_row) for step in range(1, n_row)]
 
-    def exponentials(q, i):
+    def exponentials(q, i, c):
         scores = jnp.dot(
-            bt_ref[...], a_ref[q, :, pl.ds(i * block, block)], preferred_element_type=jnp.float32
-        )
-        return jnp.exp2(scores)
+            bt_ref[pl.ds(c * block, block), :],
+            a_ref[q, :, pl.ds(i * block, block)],
+            preferred_element_type=jnp.float32,
+        )
+        return jnp.exp2(scores * alpha)
 
     def row_part(q):
         for i in range(per):
-            total = jnp.sum(exponentials(q, i).reshape(cols // 8, 8, block), axis=0)
+            total = jnp.zeros((8, block), jnp.float32)
+            for c in range(col_blocks):
+                total += jnp.sum(exponentials(q, i, c).reshape(block // 8, 8, block), axis=0)
             l_ref[q, :, pl.ds(i * block, block)] = jnp.sum(total, axis=0, keepdims=True)
 
     def col_part(q):
-        a_ref[q, bias_rows, :] = with_bias(abase[q], t_ref[q] + lift, 0).astype(jnp.bfloat16)
-        for i in range(per):
-            terms = exponentials(q, i)
-            sums_ref[...] += sum(terms[:, j : j + 128] for j in range(0, block, 128))
+        bias = (t_ref[q] + lift) * inverse
+        a_ref[q, bias_rows, :] = with_bias(abase[q], bias, 0).astype(jnp.bfloat16)
+        for c in range(col_blocks):
+            folded = None
+            for i in range(per):
+                terms = exponentials(q, i, c)
+                for j in range(0, block, 128):
+                    piece = terms[:, j : j + 128]
+                    folded = piece if folded is None else folded + piece
+            sums_ref[pl.ds(c * block, block), :] += folded
 
     def iteration(k, carry):
         def row_step(s, c2):
@@ -516,8 +525,8 @@
         wait_all(c_recv.at[k], n_row - 1, c_rsem.at[k])
         whole = jnp.sum(c_recv[k], axis=0)
         u_ref[...] = u_ref[...] + ((log2_b + lift) - lifted_log2(whole))
-        b_ref[bias_rows, :] = with_bias(bbase[...], u_ref[...], 3).astype(jnp.bfloat16)
-        bt_ref[:, changing] = b_ref[changing, :].T
+        b_ref[bias_rows, :] = with_bias(bbase[...], u_ref[...] * inverse, 3).astype(jnp.bfloat16)
+        bt_ref[...] = b_ref[...].T
         return carry
 
     lax.fori_loop(0, ITERS, iteration, 0)
@@ -561,9 +570,9 @@
         in_specs=[vmem] * 3,
         out_specs=(vmem, vmem, vmem),
         scratch_shapes=[
-            pltpu.VMEM((n_col, depth, width), bf16),
-            pltpu.VMEM((depth, cols), bf16),
-            pltpu.VMEM((cols, depth), bf16),
+            pltpu.VMEM((n_col, shallow, width), bf16),
+            pltpu.VMEM((shallow, cols), bf16),
+            pltpu.VMEM((cols, shallow), bf16),
             pltpu.VMEM((n_col, slab, width), f32),
             pltpu.VMEM((slab, cols), f32),
             pltpu.VMEM((n_col, 1, width), f32),
@@ -584,7 +593,7 @@
             collective_id=0, has_side_effects=True, vmem_limit_bytes=40 * 1024 * 1024
         ),
         cost_estimate=pl.CostEstimate(
-            flops=2 * 2 * ITERS * pairs * depth,
+            flops=2 * 2 * ITERS * pairs * shallow,
             bytes_accessed=row_blocks * dim * block * 2,
             transcendentals=2 * ITERS * pairs,
         ),

time: 164 us -> 164 us (level)
  no operation moved by 1% of the time
where the time goes in v5:
time: 164 us; the launch traced here: 163 us
  Pallas kernels  161 us (98%)
  local copies, waits for them, and re-layouts  1.84 us (1%)
    pallas_call x1, Pallas kernels, run(): pl.pallas_call(functools.partial(kernel, exact, n_row, n_col), out_shape=...  82.9 us
    pallas_call x1, Pallas kernels, run_fast(): pl.pallas_call(functools.partial(fast_kernel, n_row, n_col), out_shape=(j...  78 us

profile of v5, /device:TPU:0, one launch (start us, length us, event | category | flops | bytes accessed | tf_op | source)
XLA Modules:
  0.0 163.4 jit_solution(15708014670329649205)
XLA Ops:
  0.6 0.0 copy-start
  0.6 0.0 copy-start.1
  0.6 78.0 %shard_map.54 = (f32[16,256]{1,0:T(8,128)S(1)}, f32[4,256]{1,0:T(4,128)S(1)}, s32[1,128]{1,0:T(1,128)S(1)}) custom-call(s32[16,16]{1,0:T(8,128)} %lists_ref.1, bf16[16,64,256]{2,1,0:T(8,128)(2,1)} %x_ref.1, bf16[4,64,256]{2,1,0:T(8,128)(2,1)} %y_ref.1), custom_call_target="tpu_custom_call" | custom-call | flops 8589934592 | bytes 524288 | tf_op jit(solution)/shard_map/pallas_call | solution.py:563
  78.6 0.0 copy-start.2
  78.7 0.0 copy-done
  78.7 0.0 copy-done.1
  78.7 0.6 copy-done.2
  79.3 82.9 %conditional.1 = ((f32[16,256]{1,0:T(8,128)S(1)}, f32[4,256]{1,0:T(4,128)S(1)})) conditional(s32[]{:T(128)} %bitcast, (f32[16,256]{1,0:T(8,128)S(1)}, f32[4,256]{1,0:T(4,128)S(1)}) %tuple.14, (s32[16,16]{1,0:T(8,128)S(1)}, bf16[16,64,256]{2,1,0:T(8,128)(2,1)S(1)}, bf16[4,64,256]{2,1,0:T(8,128)(2,1)S(1)}) %tuple.28), branch_computations={%region_0.0_spmd, %region_1.0_spmd} | conditional | flops 17179869184 | bytes 524312 | solution.py:605
  79.3 82.9 %branch_1_fun.1 = (f32[16,256]{1,0:T(8,128)S(1)}, f32[4,256]{1,0:T(4,128)S(1)}, s32[1,128]{1,0:T(1,128)}) custom-call(s32[16,16]{1,0:T(8,128)S(1)} %get-tuple-element.10.lists_ref, bf16[16,64,256]{2,1,0:T(8,128)(2,1)S(1)} %get-tuple-element.11.x_ref, bf16[4,64,256]{2,1,0:T(8,128)(2,1)S(1)} %get-tuple-element.12.y_ref), custom_call_target="tpu_custom_call" | custom-call | flops 17179869184 | bytes 524288 | tf_op jit(solution)/shard_map/cond/branch_1_fun/pallas_call | solution.py:311
  162.2 0.6 copy.15
  162.9 0.6 copy.16
Async XLA Ops:
  0.6 78.1 %copy-start = (bf16[16,64,256]{2,1,0:T(8,128)(2,1)S(1)}, bf16[16,64,256]{2,1,0:T(8,128)(2,1)}, u32[]{:S(2)}) copy-start(bf16[16,64,256]{2,1,0:T(8,128)(2,1)} %x_ref.1) | copy-start | bytes 1572868
  0.6 78.1 %copy-start.1 = (bf16[4,64,256]{2,1,0:T(8,128)(2,1)S(1)}, bf16[4,64,256]{2,1,0:T(8,128)(2,1)}, u32[]{:S(2)}) copy-start(bf16[4,64,256]{2,1,0:T(8,128)(2,1)} %y_ref.1) | copy-start | bytes 393220
  78.6 0.7 copy-start.2
